TPU v7x, 512 devices: a whole 4x8x8 slice. The times are simulated.
512 devices in a mesh: dp: 8 (over x, core), centers: 64 (over z, y).
Axes of the slice: x: 4, y: 8, z: 8, core: 2. Of those that a mesh axis runs over, the one named last changes fastest.
Arguments:
- features: bfloat16 [64, 32768], P(None, 'dp'), may hold values from -8 to 8
- prices: float32 [32768], P('dp'), may hold values from -6 to 6
- slots: int32 [32768], P('dp'), may hold values from 0 to 7
- center_idx: int32 [32768], P('centers'), may hold values from 0 to 32767
- center_scale: float32 [32768], P('centers'), may hold values from 0.5 to 18
Outputs:
- coefficients: float32 [8, 32768], P(None, 'centers')
- residual: float32 [8, 32768], P(None, 'centers')
All inputs are finite; a program needn't handle non-finite values.
Results may differ from a plain program's by a relative error of at most 0.00195.
Values may be sent and summed in bfloat16 or wider, within the bound.
A program may use at most 64 MiB of HBM per device.

v0:
```python
import jax
import jax.numpy as jnp
from jax import lax
from jax.sharding import PartitionSpec as P

F = 64
SLOTS = 8
ITERS = 2


highest_prec = lax.Precision.HIGHEST
ridge_shift = 0.5
tile_rows = 512


def kernel_rows(features, center_f, center_norm, first_row, row_total):
    columns = lax.dynamic_slice_in_dim(features, first_row, row_total, 1)
    inner_prod = lax.dot_general(
        columns, center_f, (((0,), (0,)), ((), ())), preferred_element_type=jnp.float32
    )
    col32 = columns.astype(jnp.float32)
    row_norm = jnp.sum(col32 * col32, axis=0)
    return jnp.exp(-(row_norm[:, None] + center_norm[None, :] - 2.0 * inner_prod) / (2.0 * F))


def apply_rows(features, center_f, center_norm, scaled, first_row, row_total):

    def one_block(begin):
        kernel_tile = kernel_rows(features, center_f, center_norm, begin, tile_rows)
        return lax.dot_general(
            kernel_tile,
            scaled,
            (((1,), (1,)), ((), ())),
            precision=highest_prec,
            preferred_element_type=jnp.float32,
        )

    def apply_visit(turn, filled):
        return lax.dynamic_update_slice_in_dim(
            filled, one_block(first_row + turn * tile_rows), turn * tile_rows, 0
        )

    start_fill = jnp.zeros((row_total, scaled.shape[0]), jnp.float32)
    return lax.fori_loop(0, row_total // tile_rows, apply_visit, start_fill)


def fold_rows(features, center_f, center_norm, weights, first_row, summed):
    row_total = weights.shape[0]

    def fold_visit(turn, running):
        kernel_tile = kernel_rows(
            features, center_f, center_norm, first_row + turn * tile_rows, tile_rows
        )
        weight_blk = lax.dynamic_slice_in_dim(weights, turn * tile_rows, tile_rows, 0)
        return running + lax.dot_general(
            weight_blk,
            kernel_tile,
            (((0,), (0,)), ((), ())),
            precision=highest_prec,
            preferred_element_type=jnp.float32,
        )

    return lax.fori_loop(0, row_total // tile_rows, fold_visit, summed)


def group_total(partial_value):
    return lax.psum(partial_value, "dp")


def residual_norm(current):
    return lax.psum(jnp.sum(current * current, axis=1), "centers")


def per_device(features, prices, slots, center_idx, center_scale):
    row_count = features.shape[1]
    center_count = center_idx.shape[0]
    group_index = lax.axis_index("dp")
    local_idx = center_idx - group_index * row_count
    inside = (local_idx >= 0) & (local_idx < row_count)
    picked = jnp.take(features, jnp.clip(local_idx, 0, row_count - 1), axis=1)
    contrib = jnp.where(inside[None, :], picked.astype(jnp.float32), 0.0)
    center_f = lax.psum(contrib.astype(jnp.bfloat16), "dp")
    center32 = center_f.astype(jnp.float32)
    center_norm = jnp.sum(center32 * center32, axis=0)
    slot_mask = (slots[:, None] == jnp.arange(SLOTS, dtype=jnp.int32)[None, :]).astype(jnp.float32)
    all_rows = jnp.float32(row_count * lax.axis_size("dp"))
    zero_sum = jnp.zeros((SLOTS, center_count), jnp.float32)
    first_part = fold_rows(
        features, center_f, center_norm, slot_mask * prices[:, None], 0, zero_sum
    )
    target_side = center_scale[None, :] * group_total(first_part) / jnp.sqrt(all_rows)
    coefficients = jnp.zeros((SLOTS, center_count), jnp.float32)
    residual = target_side
    direction = target_side
    norm_now = residual_norm(residual)
    for iteration in range(ITERS):
        scaled = center_scale[None, :] * direction
        row_local = apply_rows(features, center_f, center_norm, scaled, 0, row_count)
        row_whole = lax.psum(row_local, "centers")
        partial_value = fold_rows(
            features, center_f, center_norm, row_whole * slot_mask, 0, zero_sum
        )
        summed = group_total(partial_value)
        applied = center_scale[None, :] * summed / all_rows + ridge_shift * direction
        curve_sum = lax.psum(jnp.sum(direction * applied, axis=1), "centers")
        step_size = norm_now / curve_sum
        coefficients = coefficients + step_size[:, None] * direction
        residual = residual - step_size[:, None] * applied
        norm_next = residual_norm(residual)
        direction = residual + (norm_next / norm_now)[:, None] * direction
        norm_now = norm_next
    return (coefficients, residual)


def solution(mesh):
    return jax.shard_map(
        per_device,
        mesh=mesh,
        in_specs=(P(None, "dp"), P("dp"), P("dp"), P("centers"), P("centers")),
        out_specs=(P(None, "centers"), P(None, "centers")),
        check_vma=False,
    )
```

profile of v0, /device:TPU:8, one launch (start us, length us, event | category | flops | bytes accessed | tf_op | source)
XLA Modules:
  0.0 929.1 jit_solution(7415717436652633034)
XLA Ops:
  7.9 1.5 copy.7
  9.5 1.3 gather_fusion
  12.4 74.0 %all-reduce.5.cloned.1.call-done = bf16[64,512]{0,1:T(8,128)(2,1)} async-done(((bf16[64,512]{0,1:T(8,128)(2,1)}), bf16[64,512]{0,1:T(8,128)(2,1)}) %all-reduce.5.cloned.1.call-update) | async-done | bytes 65552 | tf_op jit(solution)/shard_map/psum | solution.py:82
  86.4 1.1 copy.8
  87.6 8.5 while.70
  96.1 24.2 %psum.71 = f32[8,512]{1,0:T(8,128)S(1)} all-reduce(f32[8,512]{1,0:T(8,128)S(1)} %get-tuple-element.547), channel_id=1, replica_groups=mesh['dp'=8,'centers'=64] {'dp'}, use_global_device_ids=true, to_apply=%region_5.6 | all-reduce | flops 4096 | bytes 32768 | tf_op jit(solution)/shard_map/psum | solution.py:67
  120.3 11.6 %while.68 = (s32[]{:T(128)}, f32[4096,8]{0,1:T(8,128)S(1)}, bf16[64,4096]{1,0:T(8,128)(2,1)S(1)}, f32[512]{0:T(512)S(1)}, bf16[64,512]{1,0:T(8,128)(2,1)S(1)}, /...) while((s32[]{:T(128)}, f32[4096,8]{0,1:T(8,128)S(1)}, ...), condition=%wide.region_10.11_spmd, body=%wide.region_8.10_spmd.sunk | while | flops 60128772 | bytes 2332831 | solution.py:44
  120.8 1.0 convolution_dynamic-update-slice_fusion.4
  122.2 1.0 convolution_dynamic-update-slice_fusion.4
  123.7 1.0 convolution_dynamic-update-slice_fusion.4
  125.1 1.0 convolution_dynamic-update-slice_fusion.4
  126.6 1.0 convolution_dynamic-update-slice_fusion.4
  128.0 1.0 convolution_dynamic-update-slice_fusion.4
  129.5 1.0 convolution_dynamic-update-slice_fusion.4
  130.9 1.0 convolution_dynamic-update-slice_fusion.4
  132.6 148.9 %all-reduce.7.cloned.1.call-done = f32[4096,8]{0,1:T(8,128)} async-done(((f32[4096,8]{0,1:T(8,128)}), f32[4096,8]{0,1:T(8,128)}) %all-reduce.7.cloned.1.call-update) | async-done | bytes 131088 | tf_op jit(solution)/shard_map/psum | solution.py:99
  282.4 8.5 while.71
  291.0 23.6 %psum.74 = f32[8,512]{1,0:T(8,128)S(1)} all-reduce(f32[8,512]{1,0:T(8,128)S(1)} %get-tuple-element.549), channel_id=1, replica_groups=mesh['dp'=8,'centers'=64] {'dp'}, use_global_device_ids=true, to_apply=%region_15.16 | all-reduce | flops 4096 | bytes 32768 | tf_op jit(solution)/shard_map/psum | solution.py:67
  314.7 139.0 %all-reduce = (f32[8]{0:T(128)S(1)}, f32[8]{0:T(128)S(1)}) all-reduce(f32[8]{0:T(128)S(1)} %get-tuple-element.646, f32[8]{0:T(128)S(1)} %get-tuple-element.645), channel_id=1, replica_groups=mesh['dp'=8,'centers'=64] {'centers'}, use_global_device_ids=true, to_apply=%region_7.8 | all-reduce | flops 16 | bytes 128 | tf_op jit(solution)/shard_map/psum | solution.py:71
  453.9 140.9 %psum.76 = f32[8]{0:T(128)S(1)} all-reduce(f32[8]{0:T(128)S(1)} %multiply_reduce_fusion.7), channel_id=1, replica_groups=mesh['dp'=8,'centers'=64] {'centers'}, use_global_device_ids=true, to_apply=%region_19.20 | all-reduce | flops 8 | bytes 64 | tf_op jit(solution)/shard_map/psum | solution.py:71
  594.9 11.6 %while.69 = (s32[]{:T(128)}, f32[4096,8]{0,1:T(8,128)S(1)}, bf16[64,4096]{1,0:T(8,128)(2,1)S(1)}, f32[512]{0:T(512)S(1)}, bf16[64,512]{1,0:T(8,128)(2,1)S(1)}, /...) while((s32[]{:T(128)}, f32[4096,8]{0,1:T(8,128)S(1)}, ...), condition=%wide.region_22.23_spmd, body=%wide.region_20.22_spmd.sunk | while | flops 60128772 | bytes 2332831 | solution.py:44
  595.4 1.0 convolution_dynamic-update-slice_fusion.5
  596.8 1.0 convolution_dynamic-update-slice_fusion.5
  598.3 1.0 convolution_dynamic-update-slice_fusion.5
  599.7 1.0 convolution_dynamic-update-slice_fusion.5
  601.2 1.0 convolution_dynamic-update-slice_fusion.5
  602.6 1.0 convolution_dynamic-update-slice_fusion.5
  605.5 1.0 convolution_dynamic-update-slice_fusion.5
  607.2 142.5 %all-reduce.9.cloned.1.call-done = f32[4096,8]{0,1:T(8,128)} async-done(((f32[4096,8]{0,1:T(8,128)}), f32[4096,8]{0,1:T(8,128)}) %all-reduce.9.cloned.1.call-update) | async-done | bytes 131088 | tf_op jit(solution)/shard_map/psum | solution.py:99
  750.6 8.5 while.72
  759.1 23.6 %psum.78 = f32[8,512]{1,0:T(8,128)S(1)} all-reduce(f32[8,512]{1,0:T(8,128)S(1)} %get-tuple-element.551), channel_id=1, replica_groups=mesh['dp'=8,'centers'=64] {'dp'}, use_global_device_ids=true, to_apply=%region_27.28 | all-reduce | flops 4096 | bytes 32768 | tf_op jit(solution)/shard_map/psum | solution.py:67
  782.9 139.0 %psum.79 = f32[8]{0:T(128)S(1)} all-reduce(f32[8]{0:T(128)S(1)} %multiply_reduce_fusion.6), channel_id=1, replica_groups=mesh['dp'=8,'centers'=64] {'centers'}, use_global_device_ids=true, to_apply=%region_29.30 | all-reduce | flops 8 | bytes 64 | tf_op jit(solution)/shard_map/psum | solution.py:105
  (149 shorter events, 40.3 us)
Async XLA Ops:
  7.2 79.2 %all-reduce.5.cloned.1.call-start = ((), (), s32[]{:S(2)}) async-start(), calls=%async_computation | async-start | bytes 262144 | tf_op jit(solution)/shard_map/psum | solution.py:82
  7.2 0.7 copy-start.7
  9.4 2.3 copy-start.4
  9.5 2.3 copy-start.6
  10.8 76.8 %copy-start = (bf16[64,4096]{1,0:T(8,128)(2,1)S(1)}, bf16[64,4096]{1,0:T(8,128)(2,1)}, u32[]{:S(2)}) copy-start(bf16[64,4096]{1,0:T(8,128)(2,1)} %param.15) | copy-start | bytes 1572868
  11.7 0.7 copy-start.5
  11.7 269.8 %all-reduce.7.cloned.1.call-start = ((), (), s32[]{:S(2)}) async-start(), calls=%async_computation.1 | async-start | bytes 262144 | tf_op jit(solution)/shard_map/psum | solution.py:99
  86.4 1.1 copy-start.1
  131.9 0.7 copy-start.3
  132.6 617.1 %all-reduce.9.cloned.1.call-start = ((), (), s32[]{:S(2)}) async-start(), calls=%async_computation.2 | async-start | bytes 262144 | tf_op jit(solution)/shard_map/psum | solution.py:99
  606.5 0.7 copy-start.2
Sparse Core Ops, SparseCore 0:
  11.8 74.4 all-reduce.4
  132.7 148.7 all-reduce.6
  607.3 142.3 all-reduce.8
where the time goes:
time: 929 us
  blocking collectives  490 us (53%)
  waiting for transfers between devices  365 us (39%)
  matrix products  46.5 us (5%)
  between operations  13.9 us (1%)
    psum x2, waiting for transfers between devices, per_device(): row_whole = lax.psum(row_local, 'centers')  291 us
    psum x2, blocking collectives, residual_norm(): return lax.psum(jnp.sum(current * current, axis=1), 'centers')  280 us
    psum x1, blocking collectives, per_device(): curve_sum = lax.psum(jnp.sum(direction * applied, axis=1), 'centers')  139 us
    psum x1, waiting for transfers between devices, per_device(): center_f = lax.psum(contrib.astype(jnp.bfloat16), 'dp')  74 us
    psum x3, blocking collectives, group_total(): return lax.psum(partial_value, 'dp')  71.3 us
  transfers between devices with their start and end apart: 3, of which 3 were waited for; matrix products, arithmetic and copies ran while one was open for 0% of the time, Pallas kernels for 0%

commit v1 on v0

v1 whole, which is shorter than its diff:
```python
import functools
import math

import jax
import jax.numpy as jnp
from jax import lax
from jax.experimental import pallas as pl
from jax.experimental.pallas import tpu as pltpu
from jax.sharding import PartitionSpec as P

SLOTS = 8
RIDGE = 0.5
MESH = pl.DeviceIdType.MESH
BF = jnp.bfloat16
F32 = jnp.float32

CHIPS_X = 4
RING = 8
LANE = 128


def dot_nn(a, b):
    return lax.dot_general(a, b, (((1,), (0,)), ((), ())), preferred_element_type=F32)


def dot_nt(a, b):
    return lax.dot_general(a, b, (((1,), (1,)), ((), ())), preferred_element_type=F32)


def split_rows(value):
    high = value.astype(BF).astype(F32)
    rest = value - high
    middle = rest.astype(BF).astype(F32)
    return jnp.concatenate([high, middle, rest - middle], axis=0).astype(BF)


def split_sum(rows24):
    return rows24[:SLOTS] + (rows24[SLOTS : 2 * SLOTS] + rows24[2 * SLOTS :])


def column_to_row(column):
    lane = lax.broadcasted_iota(jnp.int32, (SLOTS, LANE), 1)
    sub = lax.broadcasted_iota(jnp.int32, (SLOTS, LANE), 0)
    return jnp.sum(jnp.where(lane == sub, column, 0.0), axis=0, keepdims=True)


def row_to_column(row):
    lane = lax.broadcasted_iota(jnp.int32, (SLOTS, LANE), 1)
    sub = lax.broadcasted_iota(jnp.int32, (SLOTS, LANE), 0)
    return jnp.sum(jnp.where(lane == sub, row, 0.0), axis=1, keepdims=True)


def lane_blocks(value):
    return sum(value[:, j : j + LANE] for j in range(0, value.shape[1], LANE))


def kernel(
    total_rows,
    feat, price, slots, idx, scale,
    coef_out, resid_out,
    feat_t, e_hi, e_lo, cent, a_row, g_row,
    buf_ac, buf_ax, buf_yx, buf_yc, buf_p1, buf_p2,
    send_sem, recv_sem,
):
    f_dim, rows = feat.shape
    cols = idx.shape[1]
    half_c = cols // 2
    half_n = rows // 2
    tile = 256

    dp = lax.axis_index("dp")
    cen = lax.axis_index("centers")
    x_me, core_me = dp // 2, lax.rem(dp, 2)
    z_me, y_me = cen // RING, lax.rem(cen, RING)
    mate = [(dp + 1 - 2 * core_me, cen)]
    x_peers = [(lax.rem(dp + 2 * k, 2 * CHIPS_X), cen) for k in range(1, CHIPS_X)]
    y_peers = [(dp, z_me * RING + lax.rem(y_me + k, RING)) for k in range(1, RING)]
    z_peers = [(dp, lax.rem(z_me + k, RING) * RING + y_me) for k in range(1, RING)]

    barrier = pltpu.get_barrier_semaphore()
    everyone = mate + x_peers + y_peers + z_peers
    for peer in everyone:
        pl.semaphore_signal(barrier, inc=1, device_id=peer, device_id_type=MESH)

    used = [0]

    def start(ref, peers):
        copies = []
        for peer in peers:
            j = used[0]
            used[0] += 1
            copy = pltpu.make_async_remote_copy(
                src_ref=ref, dst_ref=ref, send_sem=send_sem.at[j], recv_sem=recv_sem.at[j],
                device_id=peer, device_id_type=MESH,
            )
            copy.start()
            copies.append(copy)
        return copies

    def finish(copies):
        for copy in copies:
            copy.wait_send()
        for copy in copies:
            copy.wait_recv()

    local_idx = idx[...] - dp * rows
    picked = [jnp.zeros((f_dim, half_c), F32) for _ in range(2)]
    for t in range(0, rows, tile):
        row = lax.broadcasted_iota(jnp.int32, (tile, half_c), 0) + t
        block = feat[:, t : t + tile]
        for h in range(2):
            hot = jnp.where(row == local_idx[:, h * half_c : (h + 1) * half_c], 1.0, 0.0)
            picked[h] = picked[h] + dot_nn(block, hot.astype(BF))
    for h in range(2):
        buf_ac[h, core_me] = picked[h].astype(BF)

    slot_id = lax.broadcasted_iota(jnp.int32, (SLOTS, rows), 0)
    norm = jnp.zeros((1, rows), F32)
    for t in range(0, f_dim, 16):
        piece = feat[t : t + 16, :].astype(F32)
        norm = norm + jnp.sum(piece * piece, axis=0, keepdims=True)
    a_row[...] = jnp.exp(norm * (-1.0 / (2.0 * f_dim)))
    for t in range(0, rows, tile):
        feat_t[t : t + tile, :] = feat[:, t : t + tile].T

    pl.semaphore_wait(barrier, len(everyone))

    copies = [start(buf_ac.at[h, core_me], mate) for h in range(2)]
    later = []
    for h in range(2):
        finish(copies[h])
        buf_ax[h, x_me] = buf_ac[h, 0] + buf_ac[h, 1]
        later.append(start(buf_ax.at[h, x_me], x_peers))

    def spread(weights):
        return split_rows(jnp.where(slots[...] == slot_id, weights, 0.0))

    weights24 = spread(a_row[...] * price[...])
    factor = math.log2(math.e) / f_dim
    center_norm = []
    for h in range(2):
        finish(later[h])
        part = (buf_ax[h, 0] + buf_ax[h, 1]) + (buf_ax[h, 2] + buf_ax[h, 3])
        cent[...] = part
        part32 = part.astype(F32)
        center_norm.append(jnp.sum(part32 * part32, axis=0, keepdims=True))
        for t in range(0, rows, tile):
            inner = dot_nn(feat_t[t : t + tile, :], cent[...])
            value = jnp.exp2(inner * factor)
            high = value.astype(BF)
            e_hi[t : t + tile, h * half_c : (h + 1) * half_c] = high
            e_lo[t : t + tile, h * half_c : (h + 1) * half_c] = (value - high.astype(F32)).astype(BF)

    def fold(v24):
        return split_sum(dot_nn(v24, e_hi[...]) + dot_nn(v24, e_lo[...]))

    def over_dp(i, payload):
        buf_yx[i, x_me] = payload
        finish(start(buf_yx.at[i, x_me], x_peers))
        buf_yc[i, core_me] = (buf_yx[i, 0] + buf_yx[i, 1]) + (buf_yx[i, 2] + buf_yx[i, 3])
        finish(start(buf_yc.at[i, core_me], mate))
        return buf_yc[i, 0] + buf_yc[i, 1]

    def over_centers(i, vector, extras):
        w24 = split_rows(factor_c * vector)
        first = []
        for h in range(2):
            span = slice(h * half_n, (h + 1) * half_n)
            part = split_sum(dot_nt(w24, e_hi[span, :]) + dot_nt(w24, e_lo[span, :]))
            mask = slots[:, h * half_n : (h + 1) * half_n] == slot_id[:, :half_n]
            chosen = jnp.sum(jnp.where(mask, part, 0.0), axis=0, keepdims=True)
            place = y_me if h == 0 else z_me
            buf_p1[i, h, place, :, :half_n] = chosen
            buf_p1[i, h, place, :, half_n:] = column_to_row(extras[h])
            first.append(start(buf_p1.at[i, h, place], y_peers if h == 0 else z_peers))
        second = []
        for h in range(2):
            finish(first[h])
            place = z_me if h == 0 else y_me
            buf_p2[i, h, place] = sum_of(buf_p1, i, h)
            second.append(start(buf_p2.at[i, h, place], z_peers if h == 0 else y_peers))
        sums = []
        for h in range(2):
            finish(second[h])
            sums.append(sum_of(buf_p2, i, h))
        row = jnp.concatenate([sums[0][:, :half_n], sums[1][:, :half_n]], axis=1)
        return row, row_to_column(sums[0][:, half_n:]), row_to_column(sums[1][:, half_n:])

    def sum_of(buf, i, h):
        v = [buf[i, h, k] for k in range(RING)]
        return ((v[0] + v[1]) + (v[2] + v[3])) + ((v[4] + v[5]) + (v[6] + v[7]))

    def slot_sums(row):
        return lane_blocks(jnp.where(slots[...] == slot_id, row * row, 0.0))

    none = jnp.zeros((SLOTS, LANE), F32)
    target = over_dp(0, jnp.concatenate([fold(weights24), none], axis=1))[:, :cols]
    factor_c = scale[...] * jnp.exp(
        jnp.concatenate(center_norm, axis=1) * (-1.0 / (2.0 * f_dim))
    )
    target = factor_c * target * (1.0 / math.sqrt(total_rows))

    rr_part = jnp.sum(target * target, axis=1, keepdims=True)
    row, rr0, _ = over_centers(0, target, (rr_part, rr_part))
    g_row[...] = a_row[...] * row
    row = g_row[...]
    both = over_dp(
        1, jnp.concatenate([fold(spread(a_row[...] * row)), slot_sums(row)], axis=1)
    )
    curve = jnp.sum(both[:, cols:], axis=1, keepdims=True) * (1.0 / total_rows) + RIDGE * rr0
    applied = factor_c * both[:, :cols] * (1.0 / total_rows) + RIDGE * target
    step0 = rr0 / curve
    residual = target - step0 * applied

    rr_part = jnp.sum(residual * residual, axis=1, keepdims=True)
    rd_part = jnp.sum(residual * target, axis=1, keepdims=True)
    row, rr1, rd1 = over_centers(1, residual, (rr_part, rd_part))
    beta = rr1 / rr0
    beta_row = jnp.sum(jnp.where(slots[...] == slot_id, beta, 0.0), axis=0, keepdims=True)
    row = a_row[...] * row + beta_row * g_row[...]
    direction = residual + beta * target
    dd = rr1 + 2.0 * beta * rd1 + beta * beta * rr0
    both = over_dp(
        2, jnp.concatenate([fold(spread(a_row[...] * row)), slot_sums(row)], axis=1)
    )
    curve = jnp.sum(both[:, cols:], axis=1, keepdims=True) * (1.0 / total_rows) + RIDGE * dd
    applied = factor_c * both[:, :cols] * (1.0 / total_rows) + RIDGE * direction
    step1 = rr1 / curve
    coef_out[...] = step0 * target + step1 * direction
    resid_out[...] = residual - step1 * applied


def per_device(total_rows, features, prices, slots, center_idx, center_scale):
    f_dim, rows = features.shape
    cols = center_idx.shape[0]
    half_c, half_n = cols // 2, rows // 2
    copies = 2 * (1 + CHIPS_X - 1) + 3 * CHIPS_X + 2 * 4 * (RING - 1)
    vmem = pl.BlockSpec(memory_space=pltpu.VMEM)
    return pl.pallas_call(
        functools.partial(kernel, total_rows),
        out_shape=[jax.ShapeDtypeStruct((SLOTS, cols), F32)] * 2,
        in_specs=[vmem] * 5,
        out_specs=[vmem] * 2,
        scratch_shapes=[
            pltpu.VMEM((rows, f_dim), BF),
            pltpu.VMEM((rows, cols), BF),
            pltpu.VMEM((rows, cols), BF),
            pltpu.VMEM((f_dim, half_c), BF),
            pltpu.VMEM((1, rows), F32),
            pltpu.VMEM((1, rows), F32),
            pltpu.VMEM((2, 2, f_dim, half_c), BF),
            pltpu.VMEM((2, CHIPS_X, f_dim, half_c), BF),
            pltpu.VMEM((3, CHIPS_X, SLOTS, cols + LANE), F32),
            pltpu.VMEM((3, 2, SLOTS, cols + LANE), F32),
            pltpu.VMEM((2, 2, RING, 1, half_n + LANE), F32),
            pltpu.VMEM((2, 2, RING, 1, half_n + LANE), F32),
            pltpu.SemaphoreType.DMA((copies,)),
            pltpu.SemaphoreType.DMA((copies,)),
        ],
        compiler_params=pltpu.CompilerParams(
            collective_id=0, has_side_effects=True, vmem_limit_bytes=40 << 20
        ),
        name="cg_steps",
    )(
        features,
        prices.reshape(1, rows),
        slots.reshape(1, rows),
        center_idx.reshape(1, cols),
        center_scale.reshape(1, cols),
    )


def solution(mesh):
    def run(features, prices, slots, center_idx, center_scale):
        body = functools.partial(per_device, features.shape[1])
        return jax.shard_map(
            body,
            mesh=mesh,
            in_specs=(P(None, "dp"), P("dp"), P("dp"), P("centers"), P("centers")),
            out_specs=(P(None, "centers"), P(None, "centers")),
            check_vma=False,
        )(features, prices, slots, center_idx, center_scale)

    return run
```

time: 929 us -> 73.5 us (0.08)
  the two profiles are of different devices: /device:TPU:8 before, /device:TPU:1 now
where the time goes in v1:
time: 73.5 us; the launch traced here: 73.1 us
  Pallas kernels  68.1 us (93%)
  local copies, waits for them, and re-layouts  4.37 us (6%)
    pallas_call x1, Pallas kernels, per_device(): pl.pallas_call(functools.partial(kernel, total_rows), out_shape=[jax.Shap...  68.1 us
    unnamed x12, local copies, waits for them, and re-layouts  4.37 us

profile of v1, /device:TPU:1, one launch (start us, length us, event | category | flops | bytes accessed | tf_op | source)
XLA Modules:
  0.0 73.1 jit_solution(7371763894855807572)
XLA Ops:
  0.6 0.0 copy-start.4
  0.6 0.0 copy-start.3
  0.7 0.7 copy-done.4
  1.3 0.0 copy-done.3
  1.3 0.0 copy-start
  1.3 1.0 %copy-done = bf16[64,4096]{1,0:T(8,128)(2,1)S(1)} copy-done((bf16[64,4096]{1,0:T(8,128)(2,1)S(1)}, bf16[64,4096]{1,0:T(8,128)(2,1)}, u32[]{:S(2)}) %copy-start) | copy-done | bytes 524312
  2.4 0.0 copy-start.1
  2.4 0.7 copy-done.1
  3.1 0.0 copy-start.2
  3.1 0.7 copy-done.2
  3.8 68.1 %cg_steps.1 = (f32[8,512]{1,0:T(8,128)S(1)}, f32[8,512]{1,0:T(8,128)S(1)}) custom-call(bf16[64,4096]{1,0:T(8,128)(2,1)S(1)} %copy-done, f32[1,4096]{1,0:T(1,128)S(1)} %bitcast.4, s32[1,4096]{1,0:T(1,128)S(1)} %bitcast.5, s32[1,512]{1,0:T(1,128)S(1)} %bitcast.6, f32[1,512]{1,0:T(1,128)S(1)} %bitcast.7), custom_call_target="tpu_custom_call" | custom-call | tf_op jit(solution)/shard_map/cg_steps/pallas_call | solution.py:239
  71.9 0.6 copy.9
  72.5 0.6 copy.10
Async XLA Ops:
  0.6 0.7 copy-start.4
  0.6 0.7 copy-start.3
  1.3 1.0 %copy-start = (bf16[64,4096]{1,0:T(8,128)(2,1)S(1)}, bf16[64,4096]{1,0:T(8,128)(2,1)}, u32[]{:S(2)}) copy-start(bf16[64,4096]{1,0:T(8,128)(2,1)} %feat.1) | copy-start | bytes 1572868
  2.4 0.7 copy-start.1
  3.1 0.7 copy-start.2

commit v2 on v1

v2 whole, which is shorter than its diff:
```python
import functools
import math

import jax
import jax.numpy as jnp
from jax import lax
from jax.experimental import pallas as pl
from jax.experimental.pallas import tpu as pltpu
from jax.sharding import PartitionSpec as P

SLOTS = 8
RIDGE = 0.5
MESH = pl.DeviceIdType.MESH
BF = jnp.bfloat16
F32 = jnp.float32

RING = 8
PARTS = 4
LANE = 128


def dot_nn(a, b):
    return lax.dot_general(a, b, (((1,), (0,)), ((), ())), preferred_element_type=F32)


def dot_nt(a, b):
    return lax.dot_general(a, b, (((1,), (1,)), ((), ())), preferred_element_type=F32)


def split_rows(value):
    high = value.astype(BF).astype(F32)
    rest = value - high
    middle = rest.astype(BF).astype(F32)
    return jnp.concatenate([high, middle, rest - middle], axis=0).astype(BF)


def split_sum(rows24):
    return rows24[:SLOTS] + (rows24[SLOTS : 2 * SLOTS] + rows24[2 * SLOTS : 3 * SLOTS])


def column_to_row(column):
    lane = lax.broadcasted_iota(jnp.int32, (SLOTS, LANE), 1)
    sub = lax.broadcasted_iota(jnp.int32, (SLOTS, LANE), 0)
    return jnp.sum(jnp.where(lane == sub, column, 0.0), axis=0, keepdims=True)


def row_to_column(row):
    lane = lax.broadcasted_iota(jnp.int32, (SLOTS, LANE), 1)
    sub = lax.broadcasted_iota(jnp.int32, (SLOTS, LANE), 0)
    return jnp.sum(jnp.where(lane == sub, row, 0.0), axis=1, keepdims=True)


def lane_blocks(value):
    return sum(value[:, j : j + LANE] for j in range(0, value.shape[1], LANE))


def kernel(
    total_rows,
    feat_in, price_in, slots_in, idx_in, scale_in,
    coef_out, resid_out,
    feat, price, slots, idx, scale,
    feat_t, e_hi, e_lo, t_hi, t_lo, a_row, g_row, weights,
    buf_a, buf_y0, buf_y1, buf_p1, buf_p2,
    load_sem, send_sem, recv_sem,
):
    f_dim, rows = feat.shape
    cols = idx.shape[1]
    half = cols // 2
    part_n = rows // PARTS
    tile = 256

    dp = lax.axis_index("dp")
    cen = lax.axis_index("centers")
    z_me, y_me = cen // RING, lax.rem(cen, RING)
    dp_peers = [(lax.rem(dp + k, RING), cen) for k in range(1, RING)]
    y_peers = [(dp, z_me * RING + lax.rem(y_me + k, RING)) for k in range(1, RING)]
    z_peers = [(dp, lax.rem(z_me + k, RING) * RING + y_me) for k in range(1, RING)]

    barrier = pltpu.get_barrier_semaphore()
    everyone = dp_peers + y_peers + z_peers
    loads = [
        pltpu.make_async_copy(src, dst, load_sem.at[j])
        for j, (src, dst) in enumerate(
            ((idx_in, idx), (feat_in, feat), (slots_in, slots), (price_in, price), (scale_in, scale))
        )
    ]
    for load in loads:
        load.start()
    for peer in everyone:
        pl.semaphore_signal(barrier, inc=1, device_id=peer, device_id_type=MESH)

    used = [0]

    def start(buf, me, peers):
        j = used[0]
        used[0] += 1
        for peer in peers:
            pltpu.make_async_remote_copy(
                src_ref=buf.at[me], dst_ref=buf.at[me], send_sem=send_sem.at[j], recv_sem=recv_sem.at[j],
                device_id=peer, device_id_type=MESH,
            ).start()
        return buf, j

    def finish(handle):
        buf, j = handle
        seven = buf.at[pl.ds(0, RING - 1)]
        pltpu.make_async_copy(seven, seven, send_sem.at[j]).wait()
        pltpu.make_async_copy(seven, seven, recv_sem.at[j]).wait()

    def total(buf):
        v = [buf[k] for k in range(RING)]
        return ((v[0] + v[1]) + (v[2] + v[3])) + ((v[4] + v[5]) + (v[6] + v[7]))

    loads[0].wait()
    loads[1].wait()
    local_idx = idx[...] - dp * rows
    for h in range(2):
        picked = jnp.zeros((f_dim, half), F32)
        for t in range(0, rows, tile):
            row = lax.broadcasted_iota(jnp.int32, (tile, half), 0) + t
            hot = jnp.where(row == local_idx[:, h * half : (h + 1) * half], 1.0, 0.0)
            picked = picked + dot_nn(feat[:, t : t + tile], hot.astype(BF))
        buf_a[h, dp] = picked.astype(BF)
    for load in loads[2:]:
        load.wait()
    pl.semaphore_wait(barrier, len(everyone))

    sent = [start(buf_a.at[h], dp, dp_peers) for h in range(2)]
    for t in range(0, rows, tile):
        feat_t[t : t + tile, :] = feat[:, t : t + tile].T
    norm = jnp.zeros((1, rows), F32)
    for t in range(0, f_dim, 16):
        piece = feat[t : t + 16, :].astype(F32)
        norm = norm + jnp.sum(piece * piece, axis=0, keepdims=True)
    a_row[...] = jnp.exp(norm * (-1.0 / (2.0 * f_dim)))

    def own_slot(n):
        span = slots[:, n]
        return span == lax.broadcasted_iota(jnp.int32, (SLOTS, span.shape[1]), 0)

    def columns(h):
        return slice(h * half, (h + 1) * half)

    def auctions(q):
        return slice(q * part_n, (q + 1) * part_n)

    for q in range(PARTS):
        n = auctions(q)
        v24 = split_rows(jnp.where(own_slot(n), a_row[:, n] * price[:, n], 0.0))
        weights[:, n] = jnp.concatenate([v24.astype(F32), jnp.zeros((SLOTS, part_n), F32)], axis=0).astype(BF)

    def fold(v24, n, h):
        m = columns(h)
        return dot_nn(v24, e_hi[n, m]) + dot_nn(v24, e_lo[n, m])

    factor = math.log2(math.e) / f_dim
    centers, center_norm, sums = [], [], []
    for h in range(2):
        finish(sent[h])
        part = total(buf_a.at[h])
        part32 = part.astype(F32)
        centers.append(part)
        center_norm.append(jnp.sum(part32 * part32, axis=0, keepdims=True))
        for t in range(0, rows, tile):
            value = jnp.exp2(dot_nn(feat_t[t : t + tile, :], part) * factor)
            high = value.astype(BF)
            e_hi[t : t + tile, columns(h)] = high
            e_lo[t : t + tile, columns(h)] = (value - high.astype(F32)).astype(BF)
        buf = (buf_y0 if h == 0 else buf_y1).at[0]
        buf[dp, :, :half] = split_sum(fold(weights[...], slice(0, rows), h))
        if h == 0:
            buf[dp, :, half:] = jnp.zeros((SLOTS, LANE), F32)
        sums.append(start(buf, dp, dp_peers))

    for h in range(2):
        turned = centers[h].T
        for t in range(0, rows, tile):
            value = jnp.exp2(dot_nn(turned, feat[:, t : t + tile]) * factor)
            high = value.astype(BF)
            t_hi[columns(h), t : t + tile] = high
            t_lo[columns(h), t : t + tile] = (value - high.astype(F32)).astype(BF)
    factor_c = [
        scale[:, columns(h)] * jnp.exp(center_norm[h] * (-1.0 / (2.0 * f_dim))) for h in range(2)
    ]

    def over_centers(i, vector, extras):
        w24 = split_rows(jnp.concatenate([factor_c[h] * vector[h] for h in range(2)], axis=1))
        rings = [(y_me, y_peers), (z_me, z_peers)]
        first = []
        for q in range(PARTS):
            n = auctions(q)
            part = split_sum(dot_nn(w24, t_hi[:, n]) + dot_nn(w24, t_lo[:, n]))
            place, peers = rings[q % 2]
            buf = buf_p1.at[i, q]
            buf[place, :, :part_n] = jnp.sum(
                jnp.where(own_slot(n), part, 0.0), axis=0, keepdims=True
            )
            buf[place, :, part_n:] = column_to_row(extras[min(q, 1)])
            first.append(start(buf, place, peers))
        second = []
        for q in range(PARTS):
            finish(first[q])
            place, peers = rings[1 - q % 2]
            buf = buf_p2.at[i, q]
            buf[place] = total(buf_p1.at[i, q])
            second.append(start(buf, place, peers))
        for q in range(PARTS):
            finish(second[q])
            yield total(buf_p2.at[i, q])

    def fold_over_dp(i, parts_of_g):
        acc = [jnp.zeros((3 * SLOTS, half), F32) for _ in range(2)]
        squares = jnp.zeros((SLOTS, LANE), F32)
        sums = []
        for q, row in enumerate(parts_of_g):
            n = auctions(q)
            mask = own_slot(n)
            squares = squares + lane_blocks(jnp.where(mask, row * row, 0.0))
            v24 = split_rows(jnp.where(mask, a_row[:, n] * row, 0.0))
            for h in range(2):
                acc[h] = acc[h] + fold(v24, n, h)
                if q == PARTS - 1:
                    buf = (buf_y0 if h == 0 else buf_y1).at[i]
                    buf[dp, :, :half] = split_sum(acc[h])
                    if h == 0:
                        buf[dp, :, half:] = squares
                    sums.append(start(buf, dp, dp_peers))
        return sums

    def arrived(i, sums):
        finish(sums[0])
        both = total(buf_y0.at[i])
        finish(sums[1])
        return [both[:, :half], total(buf_y1.at[i])], jnp.sum(both[:, half:], axis=1, keepdims=True)

    def dots(u, v):
        return sum(jnp.sum(u[h] * v[h], axis=1, keepdims=True) for h in range(2))

    folded, _ = arrived(0, sums)
    target = [factor_c[h] * folded[h] * (1.0 / math.sqrt(total_rows)) for h in range(2)]

    rr_part = dots(target, target)
    rr = []

    def first_sums():
        for q, row in enumerate(over_centers(0, target, (rr_part, rr_part))):
            if q == 0:
                rr.append(row_to_column(row[:, part_n:]))
            row = a_row[:, auctions(q)] * row[:, :part_n]
            g_row[:, auctions(q)] = row
            yield row

    folded, squares = arrived(1, fold_over_dp(1, first_sums()))
    step0 = rr[0] / (squares * (1.0 / total_rows) + RIDGE * rr[0])
    residual = []
    for h in range(2):
        applied = factor_c[h] * folded[h] * (1.0 / total_rows) + RIDGE * target[h]
        residual.append(target[h] - step0 * applied)

    rr_part, rd_part = dots(residual, residual), dots(residual, target)
    rd = []

    def second_sums():
        parts = over_centers(1, residual, (rr_part, rd_part))
        held = [next(parts), next(parts)]
        rr.append(row_to_column(held[0][:, part_n:]))
        rd.append(row_to_column(held[1][:, part_n:]))
        beta = rr[1] / rr[0]
        for q in range(PARTS):
            row = held[q] if q < 2 else next(parts)
            n = auctions(q)
            beta_row = jnp.sum(jnp.where(own_slot(n), beta, 0.0), axis=0, keepdims=True)
            yield a_row[:, n] * row[:, :part_n] + beta_row * g_row[:, n]

    sums = fold_over_dp(2, second_sums())
    beta = rr[1] / rr[0]
    direction = [residual[h] + beta * target[h] for h in range(2)]
    dd = rr[1] + 2.0 * beta * rd[0] + beta * beta * rr[0]
    folded, squares = arrived(2, sums)
    step1 = rr[1] / (squares * (1.0 / total_rows) + RIDGE * dd)
    for h in range(2):
        applied = factor_c[h] * folded[h] * (1.0 / total_rows) + RIDGE * direction[h]
        coef_out[:, columns(h)] = step0 * target[h] + step1 * direction[h]
        resid_out[:, columns(h)] = residual[h] - step1 * applied


def per_device(total_rows, features, prices, slots, center_idx, center_scale):
    f_dim, rows = features.shape
    cols = center_idx.shape[0]
    half, part_n = cols // 2, rows // PARTS
    exchanges = 2 + 3 * 2 + 2 * 2 * PARTS
    vmem = pl.BlockSpec(memory_space=pltpu.VMEM)
    return pl.pallas_call(
        functools.partial(kernel, total_rows),
        out_shape=[jax.ShapeDtypeStruct((SLOTS, cols), F32)] * 2,
        in_specs=[pl.BlockSpec(memory_space=pl.ANY)] * 5,
        out_specs=[vmem] * 2,
        scratch_shapes=[
            pltpu.VMEM((f_dim, rows), BF),
            pltpu.VMEM((1, rows), F32),
            pltpu.VMEM((1, rows), jnp.int32),
            pltpu.VMEM((1, cols), jnp.int32),
            pltpu.VMEM((1, cols), F32),
            pltpu.VMEM((rows, f_dim), BF),
            pltpu.VMEM((rows, cols), BF),
            pltpu.VMEM((rows, cols), BF),
            pltpu.VMEM((cols, rows), BF),
            pltpu.VMEM((cols, rows), BF),
            pltpu.VMEM((1, rows), F32),
            pltpu.VMEM((1, rows), F32),
            pltpu.VMEM((4 * SLOTS, rows), BF),
            pltpu.VMEM((2, RING, f_dim, half), BF),
            pltpu.VMEM((3, RING, SLOTS, half + LANE), F32),
            pltpu.VMEM((3, RING, SLOTS, half), F32),
            pltpu.VMEM((2, PARTS, RING, 1, part_n + LANE), F32),
            pltpu.VMEM((2, PARTS, RING, 1, part_n + LANE), F32),
            pltpu.SemaphoreType.DMA((5,)),
            pltpu.SemaphoreType.DMA((exchanges,)),
            pltpu.SemaphoreType.DMA((exchanges,)),
        ],
        compiler_params=pltpu.CompilerParams(
            collective_id=0, has_side_effects=True, vmem_limit_bytes=50 << 20
        ),
        name="cg_steps",
    )(
        features,
        prices.reshape(1, rows),
        slots.reshape(1, rows),
        center_idx.reshape(1, cols),
        center_scale.reshape(1, cols),
    )


def solution(mesh):
    def run(features, prices, slots, center_idx, center_scale):
        body = functools.partial(per_device, features.shape[1])
        return jax.shard_map(
            body,
            mesh=mesh,
            in_specs=(P(None, "dp"), P("dp"), P("dp"), P("centers"), P("centers")),
            out_specs=(P(None, "centers"), P(None, "centers")),
            check_vma=False,
        )(features, prices, slots, center_idx, center_scale)

    return run
```

time: 73.5 us -> 66.1 us (0.90)
  Pallas kernels: 68.1 us -> 60.8 us
    pallas_call x1, Pallas kernels: 68.1 us -> 60.8 us  [per_device(): pl.pallas_call(functools.partial(kernel, total_rows), out_shape=[jax.Shap...]
where the time goes in v2:
time: 66.1 us; the launch traced here: 65.8 us
  Pallas kernels  60.8 us (92%)
  local copies, waits for them, and re-layouts  4.37 us (7%)
    pallas_call x1, Pallas kernels, per_device(): pl.pallas_call(functools.partial(kernel, total_rows), out_shape=[jax.Shap...  60.8 us
    unnamed x12, local copies, waits for them, and re-layouts  4.37 us

profile of v2, /device:TPU:1, one launch (start us, length us, event | category | flops | bytes accessed | tf_op | source)
XLA Modules:
  0.0 65.8 jit_solution(7493324236714909195)
XLA Ops:
  0.6 0.0 copy-start.4
  0.6 0.0 copy-start.3
  0.7 0.7 %copy-done.4 = f32[512]{0:T(512)S(1)} copy-done((f32[512]{0:T(512)S(1)}, f32[512]{0:T(512)}, u32[]{:S(2)}) %copy-start.4) | copy-done | bytes 2072
  1.3 0.0 copy-done.3
  1.3 0.0 copy-start
  1.3 1.0 %copy-done = bf16[64,4096]{1,0:T(8,128)(2,1)S(1)} copy-done((bf16[64,4096]{1,0:T(8,128)(2,1)S(1)}, bf16[64,4096]{1,0:T(8,128)(2,1)}, u32[]{:S(2)}) %copy-start) | copy-done | bytes 524312
  2.4 0.0 copy-start.1
  2.4 0.7 %copy-done.1 = f32[4096]{0:T(1024)S(1)} copy-done((f32[4096]{0:T(1024)S(1)}, f32[4096]{0:T(1024)}, u32[]{:S(2)}) %copy-start.1) | copy-done | bytes 16408
  3.1 0.0 copy-start.2
  3.1 0.7 %copy-done.2 = s32[4096]{0:T(1024)S(1)} copy-done((s32[4096]{0:T(1024)S(1)}, s32[4096]{0:T(1024)}, u32[]{:S(2)}) %copy-start.2) | copy-done | bytes 16408
  3.8 60.8 %cg_steps.1 = (f32[8,512]{1,0:T(8,128)S(1)}, f32[8,512]{1,0:T(8,128)S(1)}) custom-call(bf16[64,4096]{1,0:T(8,128)(2,1)S(1)} %copy-done, f32[1,4096]{1,0:T(1,128)S(1)} %bitcast.4, s32[1,4096]{1,0:T(1,128)S(1)} %bitcast.5, s32[1,512]{1,0:T(1,128)S(1)} %bitcast.6, f32[1,512]{1,0:T(1,128)S(1)} %bitcast.7), custom_call_target="tpu_custom_call" | custom-call | tf_op jit(solution)/shard_map/cg_steps/pallas_call | solution.py:293
  64.6 0.6 copy.9
  65.2 0.6 copy.10
Async XLA Ops:
  0.6 0.7 %copy-start.4 = (f32[512]{0:T(512)S(1)}, f32[512]{0:T(512)}, u32[]{:S(2)}) copy-start(f32[512]{0:T(512)} %param.9) | copy-start | bytes 6148
  0.6 0.7 %copy-start.3 = (s32[512]{0:T(512)S(1)}, s32[512]{0:T(512)}, u32[]{:S(2)}) copy-start(s32[512]{0:T(512)} %param.8) | copy-start | bytes 6148
  1.3 1.0 %copy-start = (bf16[64,4096]{1,0:T(8,128)(2,1)S(1)}, bf16[64,4096]{1,0:T(8,128)(2,1)}, u32[]{:S(2)}) copy-start(bf16[64,4096]{1,0:T(8,128)(2,1)} %feat_in.1) | copy-start | bytes 1572868
  2.4 0.7 %copy-start.1 = (f32[4096]{0:T(1024)S(1)}, f32[4096]{0:T(1024)}, u32[]{:S(2)}) copy-start(f32[4096]{0:T(1024)} %param.6) | copy-start | bytes 49156
  3.1 0.7 %copy-start.2 = (s32[4096]{0:T(1024)S(1)}, s32[4096]{0:T(1024)}, u32[]{:S(2)}) copy-start(s32[4096]{0:T(1024)} %param.7) | copy-start | bytes 49156

commit v3 on v2

--- a/solution.py
+++ b/solution.py
@@ -15,7 +15,9 @@
 F32 = jnp.float32
 
 RING = 8
-PARTS = 4
+CHIPS_X = 4
+PARTS = 8
+RR_PART, RD_PART = 1, 2
 LANE = 128
 
 
@@ -59,8 +61,8 @@
     feat_in, price_in, slots_in, idx_in, scale_in,
     coef_out, resid_out,
     feat, price, slots, idx, scale,
-    feat_t, e_hi, e_lo, t_hi, t_lo, a_row, g_row, weights,
-    buf_a, buf_y0, buf_y1, buf_p1, buf_p2,
+    feat_t, e_hi, e_lo, t_hi, t_lo, a_row, g_row, weights, first_half,
+    buf_ax, buf_ac, buf_y0, buf_y1, buf_p1, buf_p2,
     load_sem, send_sem, recv_sem,
 ):
     f_dim, rows = feat.shape
@@ -72,7 +74,10 @@
     dp = lax.axis_index("dp")
     cen = lax.axis_index("centers")
     z_me, y_me = cen // RING, lax.rem(cen, RING)
+    x_me, core_me = dp // 2, lax.rem(dp, 2)
     dp_peers = [(lax.rem(dp + k, RING), cen) for k in range(1, RING)]
+    x_peers = [(lax.rem(dp + 2 * k, RING), cen) for k in range(1, CHIPS_X)]
+    mate = [(dp + 1 - 2 * core_me, cen)]
     y_peers = [(dp, z_me * RING + lax.rem(y_me + k, RING)) for k in range(1, RING)]
     z_peers = [(dp, lax.rem(z_me + k, RING) * RING + y_me) for k in range(1, RING)]
 
@@ -99,17 +104,18 @@
                 src_ref=buf.at[me], dst_ref=buf.at[me], send_sem=send_sem.at[j], recv_sem=recv_sem.at[j],
                 device_id=peer, device_id_type=MESH,
             ).start()
-        return buf, j
+        return buf.at[pl.ds(0, len(peers))], j
 
     def finish(handle):
-        buf, j = handle
-        seven = buf.at[pl.ds(0, RING - 1)]
-        pltpu.make_async_copy(seven, seven, send_sem.at[j]).wait()
-        pltpu.make_async_copy(seven, seven, recv_sem.at[j]).wait()
-
-    def total(buf):
-        v = [buf[k] for k in range(RING)]
-        return ((v[0] + v[1]) + (v[2] + v[3])) + ((v[4] + v[5]) + (v[6] + v[7]))
+        slots_of_peers, j = handle
+        pltpu.make_async_copy(slots_of_peers, slots_of_peers, send_sem.at[j]).wait()
+        pltpu.make_async_copy(slots_of_peers, slots_of_peers, recv_sem.at[j]).wait()
+
+    def total(buf, count=RING):
+        v = [buf[k] for k in range(count)]
+        while len(v) > 1:
+            v = [v[k] + v[k + 1] for k in range(0, len(v), 2)]
+        return v[0]
 
     loads[0].wait()
     loads[1].wait()
@@ -120,12 +126,12 @@
             row = lax.broadcasted_iota(jnp.int32, (tile, half), 0) + t
             hot = jnp.where(row == local_idx[:, h * half : (h + 1) * half], 1.0, 0.0)
             picked = picked + dot_nn(feat[:, t : t + tile], hot.astype(BF))
-        buf_a[h, dp] = picked.astype(BF)
+        buf_ax[h, x_me] = picked.astype(BF)
     for load in loads[2:]:
         load.wait()
     pl.semaphore_wait(barrier, len(everyone))
 
-    sent = [start(buf_a.at[h], dp, dp_peers) for h in range(2)]
+    sent = [start(buf_ax.at[h], x_me, x_peers) for h in range(2)]
     for t in range(0, rows, tile):
         feat_t[t : t + tile, :] = feat[:, t : t + tile].T
     norm = jnp.zeros((1, rows), F32)
@@ -157,7 +163,11 @@
     centers, center_norm, sums = [], [], []
     for h in range(2):
         finish(sent[h])
-        part = total(buf_a.at[h])
+        buf_ac[h, core_me] = total(buf_ax.at[h], CHIPS_X)
+        sent[h] = start(buf_ac.at[h], core_me, mate)
+    for h in range(2):
+        finish(sent[h])
+        part = total(buf_ac.at[h], 2)
         part32 = part.astype(F32)
         centers.append(part)
         center_norm.append(jnp.sum(part32 * part32, axis=0, keepdims=True))
@@ -183,30 +193,43 @@
         scale[:, columns(h)] * jnp.exp(center_norm[h] * (-1.0 / (2.0 * f_dim))) for h in range(2)
     ]
 
-    def over_centers(i, vector, extras):
-        w24 = split_rows(jnp.concatenate([factor_c[h] * vector[h] for h in range(2)], axis=1))
+    def apply_half(w, n, h):
+        m = columns(h)
+        return split_sum(dot_nn(w, t_hi[m, n]) + dot_nn(w, t_lo[m, n]))
+
+    def over_centers(i, halves, column_of):
+        w24 = split_rows(factor_c[0] * next(halves))
+        for q in range(PARTS):
+            n = auctions(q)
+            first_half[:, n] = apply_half(w24, n, 0)
+        w24 = split_rows(factor_c[1] * next(halves))
         rings = [(y_me, y_peers), (z_me, z_peers)]
+
+        def of_part(buf, q):
+            width = part_n + LANE if q in (RR_PART, RD_PART) else part_n
+            return buf.at[i, q, :, :, pl.ds(0, width)]
+
         first = []
         for q in range(PARTS):
             n = auctions(q)
-            part = split_sum(dot_nn(w24, t_hi[:, n]) + dot_nn(w24, t_lo[:, n]))
+            part = first_half[:, n] + apply_half(w24, n, 1)
             place, peers = rings[q % 2]
-            buf = buf_p1.at[i, q]
-            buf[place, :, :part_n] = jnp.sum(
-                jnp.where(own_slot(n), part, 0.0), axis=0, keepdims=True
-            )
-            buf[place, :, part_n:] = column_to_row(extras[min(q, 1)])
+            buf = of_part(buf_p1, q)
+            chosen = jnp.sum(jnp.where(own_slot(n), part, 0.0), axis=0, keepdims=True)
+            if q in (RR_PART, RD_PART):
+                chosen = jnp.concatenate([chosen, column_to_row(column_of(q))], axis=1)
+            buf[place] = chosen
             first.append(start(buf, place, peers))
         second = []
         for q in range(PARTS):
             finish(first[q])
             place, peers = rings[1 - q % 2]
-            buf = buf_p2.at[i, q]
-            buf[place] = total(buf_p1.at[i, q])
+            buf = of_part(buf_p2, q)
+            buf[place] = total(of_part(buf_p1, q))
             second.append(start(buf, place, peers))
         for q in range(PARTS):
             finish(second[q])
-            yield total(buf_p2.at[i, q])
+            yield total(of_part(buf_p2, q))
 
     def fold_over_dp(i, parts_of_g):
         acc = [jnp.zeros((3 * SLOTS, half), F32) for _ in range(2)]
@@ -230,67 +253,83 @@
     def arrived(i, sums):
         finish(sums[0])
         both = total(buf_y0.at[i])
+        yield both[:, :half], jnp.sum(both[:, half:], axis=1, keepdims=True)
         finish(sums[1])
-        return [both[:, :half], total(buf_y1.at[i])], jnp.sum(both[:, half:], axis=1, keepdims=True)
+        yield total(buf_y1.at[i]), None
 
     def dots(u, v):
         return sum(jnp.sum(u[h] * v[h], axis=1, keepdims=True) for h in range(2))
 
-    folded, _ = arrived(0, sums)
-    target = [factor_c[h] * folded[h] * (1.0 / math.sqrt(total_rows)) for h in range(2)]
-
-    rr_part = dots(target, target)
+    target = []
+
+    def target_halves():
+        for h, (folded, _) in enumerate(arrived(0, sums)):
+            target.append(factor_c[h] * folded * (1.0 / math.sqrt(total_rows)))
+            yield target[h]
+
     rr = []
 
     def first_sums():
-        for q, row in enumerate(over_centers(0, target, (rr_part, rr_part))):
-            if q == 0:
+        parts = over_centers(0, target_halves(), lambda q: dots(target, target))
+        for q, row in enumerate(parts):
+            if q == RR_PART:
                 rr.append(row_to_column(row[:, part_n:]))
             row = a_row[:, auctions(q)] * row[:, :part_n]
             g_row[:, auctions(q)] = row
             yield row
 
-    folded, squares = arrived(1, fold_over_dp(1, first_sums()))
-    step0 = rr[0] / (squares * (1.0 / total_rows) + RIDGE * rr[0])
-    residual = []
-    for h in range(2):
-        applied = factor_c[h] * folded[h] * (1.0 / total_rows) + RIDGE * target[h]
-        residual.append(target[h] - step0 * applied)
-
-    rr_part, rd_part = dots(residual, residual), dots(residual, target)
+    sums_one = fold_over_dp(1, first_sums())
+
+    residual, steps = [], []
+
+    def residual_halves():
+        for h, (folded, squares) in enumerate(arrived(1, sums_one)):
+            if h == 0:
+                steps.append(rr[0] / (squares * (1.0 / total_rows) + RIDGE * rr[0]))
+            applied = factor_c[h] * folded * (1.0 / total_rows) + RIDGE * target[h]
+            residual.append(target[h] - steps[0] * applied)
+            yield residual[h]
+
     rd = []
 
     def second_sums():
-        parts = over_centers(1, residual, (rr_part, rd_part))
-        held = [next(parts), next(parts)]
-        rr.append(row_to_column(held[0][:, part_n:]))
-        rd.append(row_to_column(held[1][:, part_n:]))
+        parts = over_centers(
+            1, residual_halves(), lambda q: dots(residual, residual if q == RR_PART else target)
+        )
+        held = [next(parts) for _ in range(RD_PART + 1)]
+        rr.append(row_to_column(held[RR_PART][:, part_n:]))
+        rd.append(row_to_column(held[RD_PART][:, part_n:]))
         beta = rr[1] / rr[0]
         for q in range(PARTS):
-            row = held[q] if q < 2 else next(parts)
+            row = held[q] if q <= RD_PART else next(parts)
             n = auctions(q)
             beta_row = jnp.sum(jnp.where(own_slot(n), beta, 0.0), axis=0, keepdims=True)
             yield a_row[:, n] * row[:, :part_n] + beta_row * g_row[:, n]
 
-    sums = fold_over_dp(2, second_sums())
+    sums_two = fold_over_dp(2, second_sums())
     beta = rr[1] / rr[0]
     direction = [residual[h] + beta * target[h] for h in range(2)]
     dd = rr[1] + 2.0 * beta * rd[0] + beta * beta * rr[0]
-    folded, squares = arrived(2, sums)
-    step1 = rr[1] / (squares * (1.0 / total_rows) + RIDGE * dd)
-    for h in range(2):
-        applied = factor_c[h] * folded[h] * (1.0 / total_rows) + RIDGE * direction[h]
-        coef_out[:, columns(h)] = step0 * target[h] + step1 * direction[h]
-        resid_out[:, columns(h)] = residual[h] - step1 * applied
+    for h, (folded, squares) in enumerate(arrived(2, sums_two)):
+        if h == 0:
+            steps.append(rr[1] / (squares * (1.0 / total_rows) + RIDGE * dd))
+        applied = factor_c[h] * folded * (1.0 / total_rows) + RIDGE * direction[h]
+        coef_out[:, columns(h)] = steps[0] * target[h] + steps[1] * direction[h]
+        resid_out[:, columns(h)] = residual[h] - steps[1] * applied
+
+
+def hand_out(coef, resid, coef_out, resid_out):
+    coef_out[...] = coef[...]
+    resid_out[...] = resid[...]
 
 
 def per_device(total_rows, features, prices, slots, center_idx, center_scale):
     f_dim, rows = features.shape
     cols = center_idx.shape[0]
     half, part_n = cols // 2, rows // PARTS
-    exchanges = 2 + 3 * 2 + 2 * 2 * PARTS
+    exchanges = 2 * 2 + 3 * 2 + 2 * 2 * PARTS
     vmem = pl.BlockSpec(memory_space=pltpu.VMEM)
-    return pl.pallas_call(
+    both = pl.pallas_call(
         functools.partial(kernel, total_rows),
         out_shape=[jax.ShapeDtypeStruct((SLOTS, cols), F32)] * 2,
         in_specs=[pl.BlockSpec(memory_space=pl.ANY)] * 5,
@@ -309,7 +348,9 @@
             pltpu.VMEM((1, rows), F32),
             pltpu.VMEM((1, rows), F32),
             pltpu.VMEM((4 * SLOTS, rows), BF),
-            pltpu.VMEM((2, RING, f_dim, half), BF),
+            pltpu.VMEM((SLOTS, rows), F32),
+            pltpu.VMEM((2, CHIPS_X, f_dim, half), BF),
+            pltpu.VMEM((2, 2, f_dim, half), BF),
             pltpu.VMEM((3, RING, SLOTS, half + LANE), F32),
             pltpu.VMEM((3, RING, SLOTS, half), F32),
             pltpu.VMEM((2, PARTS, RING, 1, part_n + LANE), F32),
@@ -319,7 +360,7 @@
             pltpu.SemaphoreType.DMA((exchanges,)),
         ],
         compiler_params=pltpu.CompilerParams(
-            collective_id=0, has_side_effects=True, vmem_limit_bytes=50 << 20
+            collective_id=0, has_side_effects=True, vmem_limit_bytes=60 << 20
         ),
         name="cg_steps",
     )(
@@ -329,6 +370,13 @@
         center_idx.reshape(1, cols),
         center_scale.reshape(1, cols),
     )
+    return pl.pallas_call(
+        hand_out,
+        out_shape=[jax.ShapeDtypeStruct((SLOTS, cols), F32)] * 2,
+        in_specs=[vmem] * 2,
+        out_specs=[vmem] * 2,
+        name="hand_out",
+    )(*both)
 
 
 def solution(mesh):

time: 66.1 us -> 62.6 us (0.947)
  local copies, waits for them, and re-layouts: 4.37 us -> 0 us
  Pallas kernels: 60.8 us -> 61.8 us
    unnamed x12 -> x0, local copies, waits for them, and re-layouts: 4.37 us -> none
    pallas_call x0 -> x1, Pallas kernels: none -> 1.35 us  [per_device(): pl.pallas_call(hand_out, out_shape=[jax.ShapeDtypeStruct((SLOTS, cols), F...]
where the time goes in v3:
time: 62.6 us; the launch traced here: 62.4 us
  Pallas kernels  61.8 us (99%)
  between operations  0.64 us (1%)
    pallas_call x1, Pallas kernels, per_device(): pl.pallas_call(functools.partial(kernel, total_rows), out_shape=[jax.Shap...  60.4 us
    pallas_call x1, Pallas kernels, per_device(): pl.pallas_call(hand_out, out_shape=[jax.ShapeDtypeStruct((SLOTS, cols), F...  1.35 us

profile of v3, /device:TPU:1, one launch (start us, length us, event | category | flops | bytes accessed | tf_op | source)
XLA Modules:
  0.0 62.4 jit_solution(9406988489056993023)
XLA Ops:
  0.6 60.4 %cg_steps.1 = (f32[8,512]{1,0:T(8,128)}, f32[8,512]{1,0:T(8,128)}) custom-call(bf16[64,4096]{1,0:T(8,128)(2,1)} %feat_in.1, f32[1,4096]{1,0:T(1,128)} %bitcast.4, s32[1,4096]{1,0:T(1,128)} %bitcast.5, s32[1,512]{1,0:T(1,128)} %bitcast.6, f32[1,512]{1,0:T(1,128)} %bitcast.7), custom_call_target="tpu_custom_call" | custom-call | tf_op jit(solution)/shard_map/cg_steps/pallas_call | solution.py:332
  61.1 1.3 %hand_out.1 = (f32[8,512]{1,0:T(8,128)}, f32[8,512]{1,0:T(8,128)}) custom-call(f32[8,512]{1,0:T(8,128)} %get-tuple-element.4.coef, f32[8,512]{1,0:T(8,128)} %get-tuple-element.5.resid), custom_call_target="tpu_custom_call" | custom-call | tf_op jit(solution)/shard_map/hand_out/pallas_call | solution.py:373

commit v4 on v3

--- a/solution.py
+++ b/solution.py
@@ -16,6 +16,7 @@
 
 RING = 8
 CHIPS_X = 4
+FAR_FIRST = (4, 3, 5, 2, 6, 1, 7)
 PARTS = 8
 RR_PART, RD_PART = 1, 2
 LANE = 128
@@ -75,11 +76,14 @@
     cen = lax.axis_index("centers")
     z_me, y_me = cen // RING, lax.rem(cen, RING)
     x_me, core_me = dp // 2, lax.rem(dp, 2)
-    dp_peers = [(lax.rem(dp + k, RING), cen) for k in range(1, RING)]
-    x_peers = [(lax.rem(dp + 2 * k, RING), cen) for k in range(1, CHIPS_X)]
+    x_at = [lax.rem(x_me + k, CHIPS_X) * 2 for k in range(CHIPS_X)]
+    dp_peers = [(x_at[k] + 1 - core_me, cen) for k in (2, 1, 3)]
+    dp_peers[1:1] = [(x_at[2] + core_me, cen)]
+    dp_peers += [(x_at[1] + core_me, cen), (x_at[3] + core_me, cen), (dp + 1 - 2 * core_me, cen)]
+    x_peers = [(x_at[k] + core_me, cen) for k in (2, 1, 3)]
     mate = [(dp + 1 - 2 * core_me, cen)]
-    y_peers = [(dp, z_me * RING + lax.rem(y_me + k, RING)) for k in range(1, RING)]
-    z_peers = [(dp, lax.rem(z_me + k, RING) * RING + y_me) for k in range(1, RING)]
+    y_peers = [(dp, z_me * RING + lax.rem(y_me + k, RING)) for k in FAR_FIRST]
+    z_peers = [(dp, lax.rem(z_me + k, RING) * RING + y_me) for k in FAR_FIRST]
 
     barrier = pltpu.get_barrier_semaphore()
     everyone = dp_peers + y_peers + z_peers
@@ -360,21 +364,27 @@
             pltpu.SemaphoreType.DMA((exchanges,)),
         ],
         compiler_params=pltpu.CompilerParams(
-            collective_id=0, has_side_effects=True, vmem_limit_bytes=60 << 20
+            collective_id=0, has_side_effects=True, vmem_limit_bytes=48 << 20
         ),
         name="cg_steps",
     )(
-        features,
-        prices.reshape(1, rows),
-        slots.reshape(1, rows),
-        center_idx.reshape(1, cols),
-        center_scale.reshape(1, cols),
+        *(
+            pltpu.with_memory_space_constraint(array, pltpu.HBM)
+            for array in (
+                features,
+                prices.reshape(1, rows),
+                slots.reshape(1, rows),
+                center_idx.reshape(1, cols),
+                center_scale.reshape(1, cols),
+            )
+        )
     )
     return pl.pallas_call(
         hand_out,
         out_shape=[jax.ShapeDtypeStruct((SLOTS, cols), F32)] * 2,
         in_specs=[vmem] * 2,
         out_specs=[vmem] * 2,
+        compiler_params=pltpu.CompilerParams(vmem_limit_bytes=4 << 20),
         name="hand_out",
     )(*both)
 

time: 62.6 us -> 59.9 us (0.957)
  Pallas kernels: 61.8 us -> 59.1 us
    pallas_call x1, Pallas kernels: 60.4 us -> 58.5 us  [per_device(): pl.pallas_call(functools.partial(kernel, total_rows), out_shape=[jax.Shap...]
    pallas_call x1, Pallas kernels: 1.35 us -> 0.61 us  [per_device(): pl.pallas_call(hand_out, out_shape=[jax.ShapeDtypeStruct((SLOTS, cols), F...]
where the time goes in v4:
time: 59.9 us; the launch traced here: 59.7 us
  Pallas kernels  59.1 us (99%)
  between operations  0.64 us (1%)
    pallas_call x1, Pallas kernels, per_device(): pl.pallas_call(functools.partial(kernel, total_rows), out_shape=[jax.Shap...  58.5 us

profile of v4, /device:TPU:1, one launch (start us, length us, event | category | flops | bytes accessed | tf_op | source)
XLA Modules:
  0.0 59.7 jit_solution(17715796456213752615)
XLA Ops:
  0.6 58.5 %cg_steps.1 = (f32[8,512]{1,0:T(8,128)S(1)}, f32[8,512]{1,0:T(8,128)S(1)}) custom-call(bf16[64,4096]{1,0:T(8,128)(2,1)} %feat_in.1, f32[1,4096]{1,0:T(1,128)} %bitcast.4, s32[1,4096]{1,0:T(1,128)} %bitcast.5, s32[1,512]{1,0:T(1,128)} %bitcast.6, f32[1,512]{1,0:T(1,128)} %bitcast.7), custom_call_target="tpu_custom_call" | custom-call | tf_op jit(solution)/shard_map/cg_steps/pallas_call | solution.py:336
  59.1 0.6 %hand_out.1 = (f32[8,512]{1,0:T(8,128)}, f32[8,512]{1,0:T(8,128)}) custom-call(f32[8,512]{1,0:T(8,128)S(1)} %get-tuple-element.4.coef, f32[8,512]{1,0:T(8,128)S(1)} %get-tuple-element.5.resid), custom_call_target="tpu_custom_call" | custom-call | tf_op jit(solution)/shard_map/hand_out/pallas_call | solution.py:382

commit v5 on v4

--- a/solution.py
+++ b/solution.py
@@ -17,8 +17,9 @@
 RING = 8
 CHIPS_X = 4
 FAR_FIRST = (4, 3, 5, 2, 6, 1, 7)
-PARTS = 8
-RR_PART, RD_PART = 1, 2
+APPLY_PARTS, PARTS = 8, 8
+RR_IN, RD_IN = 1, 2
+RR_PART, RD_PART = RR_IN * PARTS // APPLY_PARTS, RD_IN * PARTS // APPLY_PARTS
 LANE = 128
 
 
@@ -62,7 +63,7 @@
     feat_in, price_in, slots_in, idx_in, scale_in,
     coef_out, resid_out,
     feat, price, slots, idx, scale,
-    feat_t, e_hi, e_lo, t_hi, t_lo, a_row, g_row, weights, first_half,
+    feat_t, e_hi, e_lo, t_hi, t_lo, a_row, g_row, weights,
     buf_ax, buf_ac, buf_y0, buf_y1, buf_p1, buf_p2,
     load_sem, send_sem, recv_sem,
 ):
@@ -70,6 +71,7 @@
     cols = idx.shape[1]
     half = cols // 2
     part_n = rows // PARTS
+    apply_n = rows // APPLY_PARTS
     tile = 256
 
     dp = lax.axis_index("dp")
@@ -86,7 +88,9 @@
     z_peers = [(dp, lax.rem(z_me + k, RING) * RING + y_me) for k in FAR_FIRST]
 
     barrier = pltpu.get_barrier_semaphore()
-    everyone = dp_peers + y_peers + z_peers
+    everyone = y_peers + z_peers + dp_peers
+    for peer in everyone:
+        pl.semaphore_signal(barrier, inc=1, device_id=peer, device_id_type=MESH)
     loads = [
         pltpu.make_async_copy(src, dst, load_sem.at[j])
         for j, (src, dst) in enumerate(
@@ -95,8 +99,6 @@
     ]
     for load in loads:
         load.start()
-    for peer in everyone:
-        pl.semaphore_signal(barrier, inc=1, device_id=peer, device_id_type=MESH)
 
     used = [0]
 
@@ -159,8 +161,7 @@
         v24 = split_rows(jnp.where(own_slot(n), a_row[:, n] * price[:, n], 0.0))
         weights[:, n] = jnp.concatenate([v24.astype(F32), jnp.zeros((SLOTS, part_n), F32)], axis=0).astype(BF)
 
-    def fold(v24, n, h):
-        m = columns(h)
+    def fold(v24, n, m):
         return dot_nn(v24, e_hi[n, m]) + dot_nn(v24, e_lo[n, m])
 
     factor = math.log2(math.e) / f_dim
@@ -175,13 +176,17 @@
         part32 = part.astype(F32)
         centers.append(part)
         center_norm.append(jnp.sum(part32 * part32, axis=0, keepdims=True))
+        acc = jnp.zeros((weights.shape[0], half), F32)
         for t in range(0, rows, tile):
             value = jnp.exp2(dot_nn(feat_t[t : t + tile, :], part) * factor)
             high = value.astype(BF)
+            low = (value - high.astype(F32)).astype(BF)
             e_hi[t : t + tile, columns(h)] = high
-            e_lo[t : t + tile, columns(h)] = (value - high.astype(F32)).astype(BF)
+            e_lo[t : t + tile, columns(h)] = low
+            piece = weights[:, t : t + tile]
+            acc = acc + (dot_nn(piece, high) + dot_nn(piece, low))
         buf = (buf_y0 if h == 0 else buf_y1).at[0]
-        buf[dp, :, :half] = split_sum(fold(weights[...], slice(0, rows), h))
+        buf[dp, :, :half] = split_sum(acc)
         if h == 0:
             buf[dp, :, half:] = jnp.zeros((SLOTS, LANE), F32)
         sums.append(start(buf, dp, dp_peers))
@@ -197,46 +202,61 @@
         scale[:, columns(h)] * jnp.exp(center_norm[h] * (-1.0 / (2.0 * f_dim))) for h in range(2)
     ]
 
-    def apply_half(w, n, h):
-        m = columns(h)
-        return split_sum(dot_nn(w, t_hi[m, n]) + dot_nn(w, t_lo[m, n]))
-
     def over_centers(i, halves, column_of):
-        w24 = split_rows(factor_c[0] * next(halves))
-        for q in range(PARTS):
-            n = auctions(q)
-            first_half[:, n] = apply_half(w24, n, 0)
-        w24 = split_rows(factor_c[1] * next(halves))
+        w24 = split_rows(jnp.concatenate([factor_c[h] * next(halves) for h in range(2)], axis=1))
         rings = [(y_me, y_peers), (z_me, z_peers)]
-
-        def of_part(buf, q):
-            width = part_n + LANE if q in (RR_PART, RD_PART) else part_n
-            return buf.at[i, q, :, :, pl.ds(0, width)]
+        few = min(APPLY_PARTS, PARTS)
+        joined, cut = APPLY_PARTS // few, PARTS // few
+
+        def sent_part(q):
+            return buf_p1.at[i, q, :, :, pl.ds(0, apply_n + (LANE if q in (RR_IN, RD_IN) else 0))]
+
+        def summed_part(q):
+            return buf_p2.at[i, q, :, :, pl.ds(0, part_n + (LANE if q in (RR_PART, RD_PART) else 0))]
+
+        def products(q):
+            n = slice(q * apply_n, (q + 1) * apply_n)
+            return split_sum(dot_nn(w24, t_hi[:, n]) + dot_nn(w24, t_lo[:, n]))
 
         first = []
-        for q in range(PARTS):
-            n = auctions(q)
-            part = first_half[:, n] + apply_half(w24, n, 1)
-            place, peers = rings[q % 2]
-            buf = of_part(buf_p1, q)
+        ahead = products(0)
+        for q in range(APPLY_PARTS):
+            n = slice(q * apply_n, (q + 1) * apply_n)
+            part = ahead
+            if q + 1 < APPLY_PARTS:
+                ahead = products(q + 1)
+            place, peers = rings[q // joined % 2]
+            buf = sent_part(q)
             chosen = jnp.sum(jnp.where(own_slot(n), part, 0.0), axis=0, keepdims=True)
-            if q in (RR_PART, RD_PART):
+            if q in (RR_IN, RD_IN):
                 chosen = jnp.concatenate([chosen, column_to_row(column_of(q))], axis=1)
             buf[place] = chosen
             first.append(start(buf, place, peers))
         second = []
-        for q in range(PARTS):
-            finish(first[q])
-            place, peers = rings[1 - q % 2]
-            buf = of_part(buf_p2, q)
-            buf[place] = total(of_part(buf_p1, q))
-            second.append(start(buf, place, peers))
+        for p in range(few):
+            pieces, extras = [], []
+            for q in range(p * joined, (p + 1) * joined):
+                finish(first[q])
+                row = total(sent_part(q))
+                pieces.append(row[:, :apply_n])
+                if q in (RR_IN, RD_IN):
+                    extras.append(row[:, apply_n:])
+            row = jnp.concatenate(pieces, axis=1) if joined > 1 else pieces[0]
+            place, peers = rings[1 - p % 2]
+            for k in range(cut):
+                q = p * cut + k
+                piece = row[:, k * part_n : (k + 1) * part_n]
+                if q in (RR_PART, RD_PART):
+                    piece = jnp.concatenate([piece, extras.pop(0)], axis=1)
+                buf = summed_part(q)
+                buf[place] = piece
+                second.append(start(buf, place, peers))
         for q in range(PARTS):
             finish(second[q])
-            yield total(of_part(buf_p2, q))
+            yield total(summed_part(q))
 
     def fold_over_dp(i, parts_of_g):
-        acc = [jnp.zeros((3 * SLOTS, half), F32) for _ in range(2)]
+        acc = jnp.zeros((3 * SLOTS, cols), F32)
         squares = jnp.zeros((SLOTS, LANE), F32)
         sums = []
         for q, row in enumerate(parts_of_g):
@@ -244,14 +264,15 @@
             mask = own_slot(n)
             squares = squares + lane_blocks(jnp.where(mask, row * row, 0.0))
             v24 = split_rows(jnp.where(mask, a_row[:, n] * row, 0.0))
+            if q < PARTS - 1:
+                acc = acc + fold(v24, n, slice(0, cols))
+                continue
             for h in range(2):
-                acc[h] = acc[h] + fold(v24, n, h)
-                if q == PARTS - 1:
-                    buf = (buf_y0 if h == 0 else buf_y1).at[i]
-                    buf[dp, :, :half] = split_sum(acc[h])
-                    if h == 0:
-                        buf[dp, :, half:] = squares
-                    sums.append(start(buf, dp, dp_peers))
+                buf = (buf_y0 if h == 0 else buf_y1).at[i]
+                buf[dp, :, :half] = split_sum(acc[:, columns(h)] + fold(v24, n, columns(h)))
+                if h == 0:
+                    buf[dp, :, half:] = squares
+                sums.append(start(buf, dp, dp_peers))
         return sums
 
     def arrived(i, sums):
@@ -298,7 +319,7 @@
 
     def second_sums():
         parts = over_centers(
-            1, residual_halves(), lambda q: dots(residual, residual if q == RR_PART else target)
+            1, residual_halves(), lambda q: dots(residual, residual if q == RR_IN else target)
         )
         held = [next(parts) for _ in range(RD_PART + 1)]
         rr.append(row_to_column(held[RR_PART][:, part_n:]))
@@ -330,8 +351,8 @@
 def per_device(total_rows, features, prices, slots, center_idx, center_scale):
     f_dim, rows = features.shape
     cols = center_idx.shape[0]
-    half, part_n = cols // 2, rows // PARTS
-    exchanges = 2 * 2 + 3 * 2 + 2 * 2 * PARTS
+    half, part_n, apply_n = cols // 2, rows // PARTS, rows // APPLY_PARTS
+    exchanges = 2 * 2 + 3 * 2 + 2 * (APPLY_PARTS + PARTS)
     vmem = pl.BlockSpec(memory_space=pltpu.VMEM)
     both = pl.pallas_call(
         functools.partial(kernel, total_rows),
@@ -352,12 +373,11 @@
             pltpu.VMEM((1, rows), F32),
             pltpu.VMEM((1, rows), F32),
             pltpu.VMEM((4 * SLOTS, rows), BF),
-            pltpu.VMEM((SLOTS, rows), F32),
             pltpu.VMEM((2, CHIPS_X, f_dim, half), BF),
             pltpu.VMEM((2, 2, f_dim, half), BF),
             pltpu.VMEM((3, RING, SLOTS, half + LANE), F32),
             pltpu.VMEM((3, RING, SLOTS, half), F32),
-            pltpu.VMEM((2, PARTS, RING, 1, part_n + LANE), F32),
+            pltpu.VMEM((2, APPLY_PARTS, RING, 1, apply_n + LANE), F32),
             pltpu.VMEM((2, PARTS, RING, 1, part_n + LANE), F32),
             pltpu.SemaphoreType.DMA((5,)),
             pltpu.SemaphoreType.DMA((exchanges,)),

time: 59.9 us -> 58.9 us (0.983)
  Pallas kernels: 59.1 us -> 58.2 us
    pallas_call x1, Pallas kernels: 58.5 us -> 57.5 us  [per_device(): pl.pallas_call(functools.partial(kernel, total_rows), out_shape=[jax.Shap...]
where the time goes in v5:
time: 58.9 us; the launch traced here: 58.8 us
  Pallas kernels  58.2 us (99%)
  between operations  0.64 us (1%)
    pallas_call x1, Pallas kernels, per_device(): pl.pallas_call(functools.partial(kernel, total_rows), out_shape=[jax.Shap...  57.5 us

profile of v5, /device:TPU:1, one launch (start us, length us, event | category | flops | bytes accessed | tf_op | source)
XLA Modules:
  0.0 58.8 jit_solution(18196412238134540291)
XLA Ops:
  0.6 57.5 %cg_steps.1 = (f32[8,512]{1,0:T(8,128)S(1)}, f32[8,512]{1,0:T(8,128)S(1)}) custom-call(bf16[64,4096]{1,0:T(8,128)(2,1)} %feat_in.1, f32[1,4096]{1,0:T(1,128)} %bitcast.4, s32[1,4096]{1,0:T(1,128)} %bitcast.5, s32[1,512]{1,0:T(1,128)} %bitcast.6, f32[1,512]{1,0:T(1,128)} %bitcast.7), custom_call_target="tpu_custom_call" | custom-call | tf_op jit(solution)/shard_map/cg_steps/pallas_call | solution.py:357
  58.2 0.6 %hand_out.1 = (f32[8,512]{1,0:T(8,128)}, f32[8,512]{1,0:T(8,128)}) custom-call(f32[8,512]{1,0:T(8,128)S(1)} %get-tuple-element.4.coef, f32[8,512]{1,0:T(8,128)S(1)} %get-tuple-element.5.resid), custom_call_target="tpu_custom_call" | custom-call | tf_op jit(solution)/shard_map/hand_out/pallas_call | solution.py:402
